TPU v7x, 512 devices: a whole 4x4x16 slice. The times are simulated.
512 devices in a mesh: sub: 32 (over z_lo, x, core), reg: 16 (over z_hi, y).
Axes of the slice: x: 4, y: 4, z: 16 (z_hi: 4, z_lo: 4; z = z_hi * 4 + z_lo), core: 2. Of those that a mesh axis runs over, the one named last changes fastest.
Arguments:
- right_side: float32 [32, 16, 1280, 16], P('sub', 'reg'), may hold values from -6 to 6
- tiles: bfloat16 [32, 16, 80, 128, 128], P('sub', 'reg'), may hold values from -1 to 5
- tile_list: int32 [32, 16, 80, 2], P('sub', 'reg'), may hold values from 0 to 9, as said below
- weights: float32 [32, 16, 1280], P('sub', 'reg'), may hold values from 0.15 to 0.35
- face_map: int32 [32, 16, 6], P('sub', 'reg'), may hold values from 0 to 9, as said below
- matching: int32 [32, 16, 6, 128], P('sub', 'reg'), may hold values from 0 to 127, each once within a row
- coarse_basis: bfloat16 [32, 16, 1280, 128], P('sub', 'reg'), may hold values from -0.15625 to 0.15625
- coarse_map: int32 [32, 16, 128], P('sub', 'reg'), may hold values from 0 to 2047, as said below
- coarse_inverse: float32 [16, 2048, 2048], P('reg', 'sub'), may hold values from -1 to 2, as said below
Outputs:
- solution: bfloat16 [32, 16, 1280, 16], P('sub', 'reg')
- residual: bfloat16 [32, 16, 1280, 16], P('sub', 'reg')
Inputs may be any that keep to these rules, and one draw needn't show every extreme that they name: `tile_list`: entries 0 to 9 of each subdomain's list are (b, b) for b in order; the other 70 entries are distinct off-diagonal block pairs. `face_map`: the six blocks of a subdomain are distinct. `coarse_map`: A subdomain's 128 numbers are distinct, and within a subregion every number is named by exactly two subdomains. `coarse_inverse`: symmetric in its last two dimensions.
All inputs are finite; a program needn't handle non-finite values.
Results may differ from a plain program's by a relative error of at most 0.0075.
Values may be sent and summed in bfloat16 or wider, within the bound.
A program may use at most 64 MiB of HBM per device.

v0:
```python
import jax
import jax.numpy as jnp
from jax import lax
from jax.sharding import PartitionSpec as P

SWEEPS = 3


def from_behind(shard, axis, by):
    peers = lax.axis_size(axis)
    return lax.ppermute(shard, axis, [(i, (i + by) % peers) for i in range(peers)])


def body(
    right_side,
    tiles,
    tile_list,
    weights,
    face_map,
    matching,
    coarse_basis,
    coarse_map,
    coarse_inverse,
):
    order = right_side.shape[2]
    rights = right_side.shape[3]
    tile = tiles.shape[3]
    blocks = order // tile
    target = right_side[0, 0]
    tile_block = tiles[0, 0]
    listing = tile_list[0, 0]
    scaling = weights[0, 0][:, None]
    faces_here = face_map[0, 0]
    matched = matching[0, 0]
    basis = coarse_basis[0, 0]
    own_map = coarse_map[0, 0]
    inverse_rows = coarse_inverse[0]
    block_ids = jnp.arange(blocks, dtype=jnp.int32)
    row_table = (listing[:, 0][None, :] == block_ids[:, None]).astype(jnp.float32)
    face_table = (faces_here[None, :] == block_ids[:, None]).astype(jnp.float32)
    stride = max(lax.axis_size("reg") // 4, 1)
    all_ids = lax.all_gather(own_map, "sub", axis=0, tiled=True)
    selected = jnp.take(inverse_rows, all_ids, axis=1)
    solution = jnp.zeros_like(target)
    residual = target
    for sweep in range(SWEEPS):
        low = residual.astype(jnp.bfloat16)
        local_coarse = jnp.einsum("mn,mr->nr", basis, low, preferred_element_type=jnp.float32)
        solved_rows = jnp.dot(
            selected,
            lax.all_gather(local_coarse, "sub", axis=0, tiled=True),
            precision=lax.Precision.HIGHEST,
            preferred_element_type=jnp.float32,
        )
        coarse_solution = lax.all_gather(
            solved_rows.astype(jnp.bfloat16), "sub", axis=0, tiled=True
        )
        own_values = jnp.take(coarse_solution, own_map, axis=0)
        correction = jnp.dot(basis, own_values, preferred_element_type=jnp.float32)
        solution = solution + (scaling * residual + correction)
        operator_low = solution.astype(jnp.bfloat16).reshape(blocks, tile, rights)
        picked = jnp.take(operator_low, listing[:, 1], axis=0)
        products = jnp.einsum(
            "tij,tjr->tir", tile_block, picked, preferred_element_type=jnp.float32
        )
        local = jnp.einsum("bt,tir->bir", row_table, products, precision=lax.Precision.HIGHEST)
        stacked = solution.reshape(blocks, tile, rights)
        outgoing = jnp.take(stacked, faces_here, axis=0)
        arrived = []
        for face, offset in ((0, 1), (1, -1), (2, stride), (3, -stride)):
            arrived.append(from_behind(outgoing[face ^ 1], "reg", offset))
        for face, offset in ((4, 1), (5, -1)):
            arrived.append(from_behind(outgoing[face ^ 1], "sub", offset))
        received = jnp.stack(arrived)
        permuted = jnp.take_along_axis(received, matched[:, :, None], axis=1)
        coupling = jnp.einsum("bk,kir->bir", face_table, permuted, precision=lax.Precision.HIGHEST)
        residual = target - (local - 0.5 * coupling).reshape(order, rights)
    shape = (1, 1, order, rights)
    return (
        solution.astype(jnp.bfloat16).reshape(shape),
        residual.astype(jnp.bfloat16).reshape(shape),
    )


def solution(mesh):
    placed = (
        P("sub", "reg", None, None),
        P("sub", "reg", None, None, None),
        P("sub", "reg", None, None),
        P("sub", "reg", None),
        P("sub", "reg", None),
        P("sub", "reg", None, None),
        P("sub", "reg", None, None),
        P("sub", "reg", None),
        P("reg", "sub", None),
    )
    return jax.shard_map(
        body,
        mesh=mesh,
        in_specs=placed,
        out_specs=(P("sub", "reg", None, None), P("sub", "reg", None, None)),
        check_vma=False,
    )
```

profile of v0, /device:TPU:1, one launch (start us, length us, event | category | flops | bytes accessed | tf_op | source)
XLA Modules:
  0.0 468.2 jit_solution(14664060304748137147)
XLA Ops:
  0.6 45.8 %all-gather = s32[1,1,4096]{2,1,0:T(1,128)S(1)} all-gather(s32[1,1,128]{2,1,0:T(1,128)} %param.24), channel_id=2, replica_groups=mesh['sub'=32,'reg'=16] {'sub'}, dimensions={2}, use_global_device_ids=true | all-gather | bytes 16896 | tf_op jit(solution)/shard_map/all_gather | solution.py:42
  49.1 2.4 copy.34
  52.6 38.8 %all_gather.22 = f32[4096,16]{0,1:T(8,128)S(1)} all-gather(f32[128,16]{0,1:T(8,128)S(1)} %fusion.64), channel_id=1, replica_groups=mesh['sub'=32,'reg'=16] {'sub'}, dimensions={0}, use_global_device_ids=true | all-gather | bytes 270336 | tf_op jit(solution)/shard_map/all_gather | solution.py:51
  91.5 15.4 %gather_fusion = f32[4096,64]{1,0:T(8,128)} fusion(f32[64,2048]{0,1:T(8,128)} %bitcast.250, s32[4096]{0:T(1024)S(1)} %fusion.101), kind=kCustom, calls=%fused_computation.12 | custom fusion | bytes 2113536 | tf_op jit(solution)/shard_map/jit(_take)/gather | solution.py:43
  106.9 2.9 fusion.41
  109.8 39.4 %all-gather.1 = bf16[32,64,16]{1,2,0:T(8,128)(2,1)S(1)} all-gather(bf16[1,64,16]{1,2,0:T(8,128)(2,1)S(1)} %fusion.41), channel_id=1, replica_groups=mesh['sub'=32,'reg'=16] {'sub'}, dimensions={0}, use_global_device_ids=true | all-gather | bytes 67584 | tf_op jit(solution)/shard_map/all_gather | solution.py:55
  150.2 1.8 gather_fusion.1
  154.3 3.2 collective-permute-start
  157.5 10.9 %collective-permute-start.1 = (f32[128,16]{0,1:T(8,128)S(1)}, f32[128,16]{0,1:T(8,128)}, u32[]{:S(2)}, u32[]{:S(2)}) collective-permute-start(f32[128,16]{0,1:T(8,128)S(1)} %get-tuple-element.26), channel_id=1, source_target_pairs={{0,15},{1,0},{2,1},{3,2},{4,3},{5,4},{6,5},{7,6},{8,7},{9,8},{10,9... | collective-permute-start | bytes 24584 | tf_op jit(solution)/shard_map/ppermute | solution.py:11
  168.4 6.0 %collective-permute-start.2 = (f32[128,16]{0,1:T(8,128)S(1)}, f32[128,16]{0,1:T(8,128)}, u32[]{:S(2)}, u32[]{:S(2)}) collective-permute-start(f32[128,16]{0,1:T(8,128)S(1)} %get-tuple-element.25), channel_id=1, source_target_pairs={{0,4},{1,5},{2,6},{3,7},{4,8},{5,9},{6,10},{7,11},{8,12},{9,13},{1... | collective-permute-start | bytes 24584 | tf_op jit(solution)/shard_map/ppermute | solution.py:11
  174.4 3.2 collective-permute-start.3
  177.6 2.8 collective-permute-start.4
  181.7 2.2 fusion.17
  185.1 2.0 collective-permute-start.5
  187.2 1.3 constant_dynamic-update-slice_fusion.5
  188.4 1.3 constant_dynamic-update-slice_fusion.4
  189.7 1.3 constant_dynamic-update-slice_fusion.3
  191.0 1.3 constant_dynamic-update-slice_fusion.2
  192.3 1.3 constant_dynamic-update-slice_fusion.1
  195.2 7.0 %gather_fusion.4 = f32[768,16]{1,0:T(8,128)} fusion(f32[6,128,16]{2,1,0:T(8,128)S(1)} %copy.40, s32[768]{0:T(1024)S(1)} %bitcast.246), kind=kCustom, calls=%fused_computation.3.clone | custom fusion | bytes 104448 | tf_op jit(solution)/shard_map/jit(take_along_axis)/gather | solution.py:75
  203.4 1.2 fusion.28
  204.8 43.8 %all_gather.24 = f32[4096,16]{0,1:T(8,128)S(1)} all-gather(f32[128,16]{0,1:T(8,128)S(1)} %convolution_bitcast_fusion.4), channel_id=1, replica_groups=mesh['sub'=32,'reg'=16] {'sub'}, dimensions={0}, use_global_device_ids=true | all-gather | bytes 270336 | tf_op jit(solution)/shard_map/all_gather | solution.py:51
  248.6 2.9 fusion.38
  251.4 39.9 %all-gather.2 = bf16[32,64,16]{1,2,0:T(8,128)(2,1)S(1)} all-gather(bf16[1,64,16]{1,2,0:T(8,128)(2,1)S(1)} %fusion.38), channel_id=1, replica_groups=mesh['sub'=32,'reg'=16] {'sub'}, dimensions={0}, use_global_device_ids=true | all-gather | bytes 67584 | tf_op jit(solution)/shard_map/all_gather | solution.py:55
  292.3 1.8 gather_fusion.5
  295.8 1.9 collective-permute-start.6
  297.8 9.4 %collective-permute-start.7 = (f32[128,16]{0,1:T(8,128)S(1)}, f32[128,16]{0,1:T(8,128)S(1)}, u32[]{:S(2)}, u32[]{:S(2)}) collective-permute-start(f32[128,16]{0,1:T(8,128)S(1)} %get-tuple-element.20), channel_id=1, source_target_pairs={{0,15},{1,0},{2,1},{3,2},{4,3},{5,4},{6,5},{7,6},{8,7},{9,8},{10,9... | collective-permute-start | bytes 24584 | tf_op jit(solution)/shard_map/ppermute | solution.py:11
  307.1 6.3 %collective-permute-start.8 = (f32[128,16]{0,1:T(8,128)S(1)}, f32[128,16]{0,1:T(8,128)S(1)}, u32[]{:S(2)}, u32[]{:S(2)}) collective-permute-start(f32[128,16]{0,1:T(8,128)S(1)} %get-tuple-element.19), channel_id=1, source_target_pairs={{0,4},{1,5},{2,6},{3,7},{4,8},{5,9},{6,10},{7,11},{8,12},{9,13},{1... | collective-permute-start | bytes 24584 | tf_op jit(solution)/shard_map/ppermute | solution.py:11
  313.4 2.9 collective-permute-start.9
  316.4 2.8 collective-permute-start.10
  320.0 1.5 fusion.20
  323.3 2.4 collective-permute-start.11
  326.5 1.7 collective-permute-done.11
  328.4 7.0 %gather_fusion.8 = f32[768,16]{1,0:T(8,128)} fusion(f32[6,128,16]{2,1,0:T(8,128)S(1)} %copy.47, s32[768]{0:T(1024)S(1)} %bitcast.247), kind=kCustom, calls=%fused_computation.10.clone | custom fusion | bytes 104448 | tf_op jit(solution)/shard_map/jit(take_along_axis)/gather | solution.py:75
  336.6 1.2 fusion.27
  338.1 42.4 %all_gather.26 = f32[4096,16]{0,1:T(8,128)S(1)} all-gather(f32[128,16]{0,1:T(8,128)S(1)} %convolution_bitcast_fusion.3), channel_id=1, replica_groups=mesh['sub'=32,'reg'=16] {'sub'}, dimensions={0}, use_global_device_ids=true | all-gather | bytes 270336 | tf_op jit(solution)/shard_map/all_gather | solution.py:51
  380.5 2.9 fusion.44
  383.3 40.0 %all-gather.3 = bf16[32,64,16]{1,2,0:T(8,128)(2,1)S(1)} all-gather(bf16[1,64,16]{1,2,0:T(8,128)(2,1)S(1)} %fusion.44), channel_id=1, replica_groups=mesh['sub'=32,'reg'=16] {'sub'}, dimensions={0}, use_global_device_ids=true | all-gather | bytes 67584 | tf_op jit(solution)/shard_map/all_gather | solution.py:55
  424.3 1.8 gather_fusion.9
  427.8 1.9 collective-permute-start.12
  429.7 9.4 %collective-permute-start.13 = (f32[128,16]{0,1:T(8,128)S(1)}, f32[128,16]{0,1:T(8,128)S(1)}, u32[]{:S(2)}, u32[]{:S(2)}) collective-permute-start(f32[128,16]{0,1:T(8,128)S(1)} %get-tuple-element.14), channel_id=1, source_target_pairs={{0,15},{1,0},{2,1},{3,2},{4,3},{5,4},{6,5},{7,6},{8,7},{9,8},{10,9... | collective-permute-start | bytes 24584 | tf_op jit(solution)/shard_map/ppermute | solution.py:11
  439.1 6.3 %collective-permute-start.14 = (f32[128,16]{0,1:T(8,128)S(1)}, f32[128,16]{0,1:T(8,128)S(1)}, u32[]{:S(2)}, u32[]{:S(2)}) collective-permute-start(f32[128,16]{0,1:T(8,128)S(1)} %get-tuple-element.13), channel_id=1, source_target_pairs={{0,4},{1,5},{2,6},{3,7},{4,8},{5,9},{6,10},{7,11},{8,12},{9,13},{1... | collective-permute-start | bytes 24584 | tf_op jit(solution)/shard_map/ppermute | solution.py:11
  445.4 2.9 collective-permute-start.15
  448.3 2.8 collective-permute-start.16
  451.9 1.5 fusion.23
  453.9 2.4 collective-permute-start.17
  456.4 2.5 collective-permute-done.17
  459.1 7.0 %gather_fusion.12 = f32[768,16]{1,0:T(8,128)} fusion(f32[6,128,16]{2,1,0:T(8,128)S(1)} %copy.54, s32[768]{0:T(1024)S(1)} %bitcast.248), kind=kCustom, calls=%fused_computation.11.clone | custom fusion | bytes 104448 | tf_op jit(solution)/shard_map/jit(take_along_axis)/gather | solution.py:75
  (133 shorter events, 26.3 us)
Async XLA Ops:
  0.6 181.1 %copy-start = (bf16[1,1,80,128,128]{4,3,2,1,0:T(8,128)(2,1)S(1)}, bf16[1,1,80,128,128]{4,3,2,1,0:T(8,128)(2,1)}, u32[]{:S(2)}) copy-start(bf16[1,1,80,128,128]{4,3,2,1,0:T(8,128)(2,1)} %param.18) | copy-start | bytes 7864324
  47.8 104.3 %copy-start.15 = (pred[128]{0:T(512)(128)(4,1)}, pred[128]{0:T(512)(128)(4,1)S(1)}, u32[]{:S(2)}) copy-start(pred[128]{0:T(512)(128)(4,1)S(1)} %compare_and_fusion.4) | copy-start | bytes 388
  49.1 104.5 %copy-start.12 = (pred[6]{0:T(512)(128)(4,1)}, pred[6]{0:T(512)(128)(4,1)S(1)}, u32[]{:S(2)}) copy-start(pred[6]{0:T(512)(128)(4,1)S(1)} %compare_and_fusion.2) | copy-start | bytes 22
  106.9 45.1 %copy-start.9 = (f32[1,1,1280]{2,1,0:T(1,128)S(1)}, f32[1,1,1280]{2,1,0:T(1,128)}, u32[]{:S(2)}) copy-start(f32[1,1,1280]{2,1,0:T(1,128)} %param.20) | copy-start | bytes 15364
  106.9 45.1 %copy-start.1 = (bf16[1,1,1280,128]{3,2,1,0:T(8,128)(2,1)S(1)}, bf16[1,1,1280,128]{3,2,1,0:T(8,128)(2,1)}, u32[]{:S(2)}) copy-start(bf16[1,1,1280,128]{3,2,1,0:T(8,128)(2,1)} %param.23) | copy-start | bytes 983044
  106.9 45.2 %copy-start.2 = (f32[1,1,1280,16]{2,3,1,0:T(8,128)S(1)}, f32[1,1,1280,16]{2,3,1,0:T(8,128)}, u32[]{:S(2)}) copy-start(f32[1,1,1280,16]{2,3,1,0:T(8,128)} %param.17) | copy-start | bytes 245764
  106.9 45.5 %copy-start.23 = (s32[1,1,80,2]{2,3,1,0:T(2,128)S(1)}, s32[1,1,80,2]{2,3,1,0:T(2,128)}, u32[]{:S(2)}) copy-start(s32[1,1,80,2]{2,3,1,0:T(2,128)} %param.19) | copy-start | bytes 1924
  106.9 74.1 %copy-start.5 = (s32[1,1,6,128]{3,1,2,0:T(1,128)S(1)}, s32[1,1,6,128]{3,1,2,0:T(1,128)}, u32[]{:S(2)}) copy-start(s32[1,1,6,128]{3,1,2,0:T(1,128)} %param.22) | copy-start | bytes 9220
  153.0 28.7 %copy-start.7 = (s32[1024]{0:T(1024)}, s32[1024]{0:T(1024)S(1)}, u32[]{:S(2)}) copy-start(s32[1024]{0:T(1024)S(1)} %get-tuple-element.28) | copy-start | bytes 12292
  153.0 28.7 %copy-start.8 = (s32[1024]{0:T(1024)}, s32[1024]{0:T(1024)S(1)}, u32[]{:S(2)}) copy-start(s32[1024]{0:T(1024)S(1)} %get-tuple-element.29) | copy-start | bytes 12292
  154.3 30.9 %collective-permute-start = (f32[128,16]{0,1:T(8,128)}, f32[128,16]{0,1:T(8,128)}, u32[]{:S(2)}, u32[]{:S(2)}) collective-permute-start(f32[128,16]{0,1:T(8,128)} %get-tuple-element.27), channel_id=1, source_target_pairs={{0,1},{1,2},{2,3},{3,4},{4,5},{5,6},{6,7},{7,8},{8,9},{9,10},{10,1... | collective-permute-start | bytes 24584 | tf_op jit(solution)/shard_map/ppermute | solution.py:11
  157.5 31.0 %collective-permute-start.1 = (f32[128,16]{0,1:T(8,128)S(1)}, f32[128,16]{0,1:T(8,128)}, u32[]{:S(2)}, u32[]{:S(2)}) collective-permute-start(f32[128,16]{0,1:T(8,128)S(1)} %get-tuple-element.26), channel_id=1, source_target_pairs={{0,15},{1,0},{2,1},{3,2},{4,3},{5,4},{6,5},{7,6},{8,7},{9,8},{10,9... | collective-permute-start | bytes 24584 | tf_op jit(solution)/shard_map/ppermute | solution.py:11
  168.4 21.4 %collective-permute-start.2 = (f32[128,16]{0,1:T(8,128)S(1)}, f32[128,16]{0,1:T(8,128)}, u32[]{:S(2)}, u32[]{:S(2)}) collective-permute-start(f32[128,16]{0,1:T(8,128)S(1)} %get-tuple-element.25), channel_id=1, source_target_pairs={{0,4},{1,5},{2,6},{3,7},{4,8},{5,9},{6,10},{7,11},{8,12},{9,13},{1... | collective-permute-start | bytes 24584 | tf_op jit(solution)/shard_map/ppermute | solution.py:11
  174.4 16.7 %collective-permute-start.3 = (f32[128,16]{0,1:T(8,128)S(1)}, f32[128,16]{0,1:T(8,128)}, u32[]{:S(2)}, u32[]{:S(2)}) collective-permute-start(f32[128,16]{0,1:T(8,128)S(1)} %get-tuple-element.24), channel_id=1, source_target_pairs={{0,12},{1,13},{2,14},{3,15},{4,0},{5,1},{6,2},{7,3},{8,4},{9,5},{1... | collective-permute-start | bytes 24584 | tf_op jit(solution)/shard_map/ppermute | solution.py:11
  177.6 14.7 %collective-permute-start.4 = (f32[128,16]{0,1:T(8,128)S(1)}, f32[128,16]{0,1:T(8,128)}, u32[]{:S(2)}, u32[]{:S(2)}) collective-permute-start(f32[128,16]{0,1:T(8,128)S(1)} %get-tuple-element.23), channel_id=1, source_target_pairs={{0,16},{16,32},{32,48},{48,64},{64,80},{80,96},{96,112},{112,128},... | collective-permute-start | bytes 24584 | tf_op jit(solution)/shard_map/ppermute | solution.py:11
  181.7 2.2 copy-start.18
  185.1 8.5 %collective-permute-start.5 = (f32[128,16]{0,1:T(8,128)S(1)}, f32[128,16]{0,1:T(8,128)S(1)}, u32[]{:S(2)}, u32[]{:S(2)}) collective-permute-start(f32[128,16]{0,1:T(8,128)S(1)} %get-tuple-element.22), channel_id=1, source_target_pairs={{0,496},{16,0},{32,16},{48,32},{64,48},{80,64},{96,80},{112,96},{1... | collective-permute-start | bytes 24584 | tf_op jit(solution)/shard_map/ppermute | solution.py:11
  195.2 8.2 %copy-start.10 = (s32[1,1,6]{2,1,0:T(1,128)S(1)}, s32[1,1,6]{2,1,0:T(1,128)}, u32[]{:S(2)}) copy-start(s32[1,1,6]{2,1,0:T(1,128)} %param.21) | copy-start | bytes 76
  204.6 89.5 %copy-start.16 = (pred[128]{0:T(512)(128)(4,1)S(1)}, pred[128]{0:T(512)(128)(4,1)}, u32[]{:S(2)}) copy-start(pred[128]{0:T(512)(128)(4,1)} %copy-done.15) | copy-start | bytes 388
  248.6 47.2 %copy-start.13 = (pred[6]{0:T(512)(128)(4,1)S(1)}, pred[6]{0:T(512)(128)(4,1)}, u32[]{:S(2)}) copy-start(pred[6]{0:T(512)(128)(4,1)} %copy-done.12) | copy-start | bytes 22
  294.4 0.6 copy-start.3
  295.8 26.9 %collective-permute-start.6 = (f32[128,16]{0,1:T(8,128)S(1)}, f32[128,16]{0,1:T(8,128)S(1)}, u32[]{:S(2)}, u32[]{:S(2)}) collective-permute-start(f32[128,16]{0,1:T(8,128)S(1)} %get-tuple-element.21), channel_id=1, source_target_pairs={{0,1},{1,2},{2,3},{3,4},{4,5},{5,6},{6,7},{7,8},{8,9},{9,10},{10,1... | collective-permute-start | bytes 24584 | tf_op jit(solution)/shard_map/ppermute | solution.py:11
  297.8 28.7 %collective-permute-start.7 = (f32[128,16]{0,1:T(8,128)S(1)}, f32[128,16]{0,1:T(8,128)S(1)}, u32[]{:S(2)}, u32[]{:S(2)}) collective-permute-start(f32[128,16]{0,1:T(8,128)S(1)} %get-tuple-element.20), channel_id=1, source_target_pairs={{0,15},{1,0},{2,1},{3,2},{4,3},{5,4},{6,5},{7,6},{8,7},{9,8},{10,9... | collective-permute-start | bytes 24584 | tf_op jit(solution)/shard_map/ppermute | solution.py:11
  307.1 19.3 %collective-permute-start.8 = (f32[128,16]{0,1:T(8,128)S(1)}, f32[128,16]{0,1:T(8,128)S(1)}, u32[]{:S(2)}, u32[]{:S(2)}) collective-permute-start(f32[128,16]{0,1:T(8,128)S(1)} %get-tuple-element.19), channel_id=1, source_target_pairs={{0,4},{1,5},{2,6},{3,7},{4,8},{5,9},{6,10},{7,11},{8,12},{9,13},{1... | collective-permute-start | bytes 24584 | tf_op jit(solution)/shard_map/ppermute | solution.py:11
  313.4 13.0 %collective-permute-start.9 = (f32[128,16]{0,1:T(8,128)S(1)}, f32[128,16]{0,1:T(8,128)S(1)}, u32[]{:S(2)}, u32[]{:S(2)}) collective-permute-start(f32[128,16]{0,1:T(8,128)S(1)} %get-tuple-element.18), channel_id=1, source_target_pairs={{0,12},{1,13},{2,14},{3,15},{4,0},{5,1},{6,2},{7,3},{8,4},{9,5},{1... | collective-permute-start | bytes 24584 | tf_op jit(solution)/shard_map/ppermute | solution.py:11
  316.4 3.6 copy-start.21
  316.4 10.1 %collective-permute-start.10 = (f32[128,16]{0,1:T(8,128)S(1)}, f32[128,16]{0,1:T(8,128)S(1)}, u32[]{:S(2)}, u32[]{:S(2)}) collective-permute-start(f32[128,16]{0,1:T(8,128)S(1)} %get-tuple-element.17), channel_id=1, source_target_pairs={{0,16},{16,32},{32,48},{48,64},{64,80},{80,96},{96,112},{112,128},... | collective-permute-start | bytes 24584 | tf_op jit(solution)/shard_map/ppermute | solution.py:11
  320.0 1.5 copy-start.19
  322.7 0.6 copy-start.6
  323.3 5.0 %collective-permute-start.11 = (f32[128,16]{0,1:T(8,128)S(1)}, f32[128,16]{0,1:T(8,128)S(1)}, u32[]{:S(2)}, u32[]{:S(2)}) collective-permute-start(f32[128,16]{0,1:T(8,128)S(1)} %get-tuple-element.16), channel_id=1, source_target_pairs={{0,496},{16,0},{32,16},{48,32},{64,48},{80,64},{96,80},{112,96},{1... | collective-permute-start | bytes 24584 | tf_op jit(solution)/shard_map/ppermute | solution.py:11
  328.4 8.2 %copy-start.11 = (s32[1,1,6]{2,1,0:T(1,128)S(1)}, s32[1,1,6]{2,1,0:T(1,128)}, u32[]{:S(2)}) copy-start(s32[1,1,6]{2,1,0:T(1,128)} %param.21) | copy-start | bytes 76
  337.9 88.2 %copy-start.4 = (f32[1280,16]{0,1:T(8,128)S(1)}, f32[1280,16]{0,1:T(8,128)}, u32[]{:S(2)}) copy-start(f32[1280,16]{0,1:T(8,128)} %copy-done.3) | copy-start | bytes 245764
  337.9 88.2 %copy-start.17 = (pred[128]{0:T(512)(128)(4,1)S(1)}, pred[128]{0:T(512)(128)(4,1)}, u32[]{:S(2)}) copy-start(pred[128]{0:T(512)(128)(4,1)} %copy-done.15) | copy-start | bytes 388
  380.5 47.2 %copy-start.14 = (pred[6]{0:T(512)(128)(4,1)S(1)}, pred[6]{0:T(512)(128)(4,1)}, u32[]{:S(2)}) copy-start(pred[6]{0:T(512)(128)(4,1)} %copy-done.12) | copy-start | bytes 22
  427.8 26.1 %collective-permute-start.12 = (f32[128,16]{0,1:T(8,128)S(1)}, f32[128,16]{0,1:T(8,128)S(1)}, u32[]{:S(2)}, u32[]{:S(2)}) collective-permute-start(f32[128,16]{0,1:T(8,128)S(1)} %get-tuple-element.15), channel_id=1, source_target_pairs={{0,1},{1,2},{2,3},{3,4},{4,5},{5,6},{6,7},{7,8},{8,9},{9,10},{10,1... | collective-permute-start | bytes 24584 | tf_op jit(solution)/shard_map/ppermute | solution.py:11
  429.7 26.6 %collective-permute-start.13 = (f32[128,16]{0,1:T(8,128)S(1)}, f32[128,16]{0,1:T(8,128)S(1)}, u32[]{:S(2)}, u32[]{:S(2)}) collective-permute-start(f32[128,16]{0,1:T(8,128)S(1)} %get-tuple-element.14), channel_id=1, source_target_pairs={{0,15},{1,0},{2,1},{3,2},{4,3},{5,4},{6,5},{7,6},{8,7},{9,8},{10,9... | collective-permute-start | bytes 24584 | tf_op jit(solution)/shard_map/ppermute | solution.py:11
  439.1 17.2 %collective-permute-start.14 = (f32[128,16]{0,1:T(8,128)S(1)}, f32[128,16]{0,1:T(8,128)S(1)}, u32[]{:S(2)}, u32[]{:S(2)}) collective-permute-start(f32[128,16]{0,1:T(8,128)S(1)} %get-tuple-element.13), channel_id=1, source_target_pairs={{0,4},{1,5},{2,6},{3,7},{4,8},{5,9},{6,10},{7,11},{8,12},{9,13},{1... | collective-permute-start | bytes 24584 | tf_op jit(solution)/shard_map/ppermute | solution.py:11
  445.4 11.0 %collective-permute-start.15 = (f32[128,16]{0,1:T(8,128)S(1)}, f32[128,16]{0,1:T(8,128)S(1)}, u32[]{:S(2)}, u32[]{:S(2)}) collective-permute-start(f32[128,16]{0,1:T(8,128)S(1)} %get-tuple-element.12), channel_id=1, source_target_pairs={{0,12},{1,13},{2,14},{3,15},{4,0},{5,1},{6,2},{7,3},{8,4},{9,5},{1... | collective-permute-start | bytes 24584 | tf_op jit(solution)/shard_map/ppermute | solution.py:11
  448.3 8.1 %collective-permute-start.16 = (f32[128,16]{0,1:T(8,128)S(1)}, f32[128,16]{0,1:T(8,128)S(1)}, u32[]{:S(2)}, u32[]{:S(2)}) collective-permute-start(f32[128,16]{0,1:T(8,128)S(1)} %get-tuple-element.11), channel_id=1, source_target_pairs={{0,16},{16,32},{32,48},{48,64},{64,80},{80,96},{96,112},{112,128},... | collective-permute-start | bytes 24584 | tf_op jit(solution)/shard_map/ppermute | solution.py:11
  451.1 0.8 copy-start.22
  451.9 1.5 copy-start.20
  453.9 5.0 %collective-permute-start.17 = (f32[128,16]{0,1:T(8,128)S(1)}, f32[128,16]{0,1:T(8,128)S(1)}, u32[]{:S(2)}, u32[]{:S(2)}) collective-permute-start(f32[128,16]{0,1:T(8,128)S(1)} %get-tuple-element.10), channel_id=1, source_target_pairs={{0,496},{16,0},{32,16},{48,32},{64,48},{80,64},{96,80},{112,96},{1... | collective-permute-start | bytes 24584 | tf_op jit(solution)/shard_map/ppermute | solution.py:11
where the time goes:
time: 472 us; the launch traced here: 468 us
  blocking collectives  290 us (61%)
  starting transfers between devices  79.5 us (17%)
  local copies, waits for them, and re-layouts  66.4 us (14%)
  matrix products  21.9 us (5%)
  other arithmetic  4.82 us (1%)
    all_gather x3, blocking collectives, body(): lax.all_gather(local_coarse, 'sub', axis=0, tiled=True)  125 us
    all_gather x3, blocking collectives, body(): lax.all_gather(solved_rows.astype(jnp.bfloat16), 'sub', axis=0, tiled=True)  119 us
    ppermute x18, starting transfers between devices, from_behind(): lax.ppermute(shard, axis, [(i, (i + by) % peers) for i in range(peers)])  79.5 us
    all_gather x1, blocking collectives, body(): all_ids = lax.all_gather(own_map, 'sub', axis=0, tiled=True)  45.8 us
    gather x6, local copies, waits for them, and re-layouts, body(): permuted = jnp.take_along_axis(received, matched[:, :, None], axis=1)  24.5 us
    gather x1, local copies, waits for them, and re-layouts, body(): selected = jnp.take(inverse_rows, all_ids, axis=1)  15.4 us
    unnamed x68, local copies, waits for them, and re-layouts  13.9 us
  transfers between devices with their start and end apart: 18, of which 2 were waited for; matrix products, arithmetic and copies ran while one was open for 4% of the time, Pallas kernels for 0%

commit v1 on v0

v1 whole, which is shorter than its diff:
```python
import functools

import jax
import jax.numpy as jnp
from jax import lax
from jax.experimental import pallas as pl
from jax.experimental.pallas import tpu as pltpu
from jax.sharding import PartitionSpec as P

SWEEPS = 3
MESH = pl.DeviceIdType.MESH
LANES = 128


def dot_nt(a, b):
    return lax.dot_general(a, b, (((1,), (1,)), ((), ())), preferred_element_type=jnp.float32)


def lanes_of(x, ids):
    ids = jnp.broadcast_to(ids, x.shape)
    return jnp.take_along_axis(x, ids, axis=1, mode="promise_in_bounds")


def split(x):
    high = x.astype(jnp.bfloat16)
    return high, (x - high.astype(jnp.float32)).astype(jnp.bfloat16)


def kernel(
    subs,
    regs,
    rhs_h,
    tiles_h,
    list_h,
    weights_h,
    faces_s,
    match_h,
    basis_h,
    map_h,
    inverse_h,
    solution_o,
    residual_o,
    rhs,
    tiles,
    listing,
    weights,
    match,
    basis,
    basis_t,
    own_map,
    inverse,
    dense,
    selected,
    place,
    place_s,
    ids,
    coarse,
    partial,
    solved,
    low,
    faces_out,
    faces_in,
    permuted,
    u_ref,
    r_ref,
    local_sem,
    place_sem,
    inverse_sem,
    ids_sem,
    coarse_sem,
    partial_sem,
    solved_sem,
    face_sem,
):
    rights, order = rhs.shape
    blocks = order // LANES
    listed = tiles_h.shape[0]
    held = inverse_h.shape[0]
    chips = subs // 2
    peers = chips - 1
    stride = max(regs // 4, 1)
    i, j = lax.axis_index("sub"), lax.axis_index("reg")
    chip, core = i // 2, i % 2
    mate = i + 1 - 2 * core
    after, before = (i + 1) % subs, (i + subs - 1) % subs
    apart = (i + subs - 1 + 2 * core) % subs

    def peer(m):
        return ((chip + m + 1) % chips) * 2 + core

    def send(src, dst, sems, to_sub, to_reg):
        pltpu.make_async_remote_copy(
            src_ref=src, dst_ref=dst, send_sem=sems.at[0], recv_sem=sems.at[1],
            device_id=(to_sub, to_reg), device_id_type=MESH,
        ).start()

    def waiter(ref, sems):
        return pltpu.make_async_remote_copy(
            src_ref=ref, dst_ref=ref, send_sem=sems.at[0], recv_sem=sems.at[1],
            device_id=(mate, j), device_id_type=MESH,
        )

    loads = [
        (map_h, own_map),
        (basis_h, basis),
        (rhs_h, rhs),
        (inverse_h, inverse.at[core]),
        (list_h, listing),
        (tiles_h, tiles.at[pl.ds(0, listed)]),
        (weights_h, weights),
        (match_h, match),
    ]
    loads = [pltpu.make_async_copy(a, b, local_sem.at[n]) for n, (a, b) in enumerate(loads)]
    for load in loads:
        load.start()

    with jax.named_scope("greet"):
        barrier = pltpu.get_barrier_semaphore()

        def greet(to_sub, to_reg):
            pl.semaphore_signal(barrier, inc=1, device_id=(to_sub, to_reg), device_id_type=MESH)

        def greet_peer(m, carry):
            greet(peer(m), j)
            return carry

        for by in (1, regs - 1, stride, regs - stride):
            greet(i, (j + by) % regs)
        lax.fori_loop(0, peers, greet_peer, 0)
        greet(mate, j)
        greet(apart, j)
        pl.semaphore_wait(barrier, peers + 6)

    def to_peers(src, box, sems):
        def one(m, carry):
            send(src, box.at[m], sems, peer(m), j)
            return carry

        lax.fori_loop(0, peers, one, 0)

    def send_coarse(k):
        now = lax.dot_general(
            r_ref[...].astype(jnp.bfloat16), basis[...], (((1,), (0,)), ((), ())),
            preferred_element_type=jnp.float32,
        )
        high, rest = split(now)
        coarse[k, peers, 0:rights] = high
        if coarse.shape[2] > rights:
            coarse[k, peers, rights:] = rest
        to_peers(coarse.at[k, peers], coarse.at[k], coarse_sem.at[k])

    with jax.named_scope("first_sends"):
        send(inverse_h, inverse.at[core], inverse_sem, mate, j)
        loads[0].wait()
        ids[peers] = own_map[...]
        to_peers(ids.at[peers], ids, ids_sem)
        loads[1].wait()
        loads[2].wait()
        r_ref[...] = rhs[...]
        u_ref[...] = jnp.zeros_like(u_ref)
        send_coarse(0)

    with jax.named_scope("where_tiles"):
        tiles[listed] = jnp.zeros_like(tiles[listed])
        permuted[6] = jnp.zeros_like(permuted[6])
        loads[4].wait()
        pair = listing[0:1, :] * blocks + listing[1:2, :]
        shape = (LANES, listed)
        hit = lax.broadcasted_iota(jnp.int32, shape, 0) == jnp.broadcast_to(pair, shape)
        number = lax.broadcasted_iota(jnp.int32, shape, 1)
        found = jnp.min(jnp.where(hit, number, listed), axis=1, keepdims=True)
        place[...] = jnp.broadcast_to(found, (LANES, LANES)).T[0:1]
        to_scalars = pltpu.make_async_copy(place, place_s, place_sem)
        to_scalars.start()
        for b in range(blocks):
            basis_t[:, b * LANES : (b + 1) * LANES] = basis[b * LANES : (b + 1) * LANES, :].T
        to_scalars.wait()

    with jax.named_scope("select"):
        loads[3].wait()
        waiter(inverse.at[1 - core], inverse_sem).wait_recv()
        waiter(ids.at[pl.ds(0, peers)], ids_sem).wait_recv()

        def select(s, carry):
            numbers = ids[s]
            lane, block = numbers % LANES, numbers // LANES
            for half in range(2):
                chosen = jnp.zeros((held, LANES), jnp.float32)
                for b in range(chips):
                    source = inverse[half, :, b * LANES : (b + 1) * LANES]
                    chosen = jnp.where(block == b, lanes_of(source, lane), chosen)
                high, rest = split(chosen)
                columns = pl.ds(pl.multiple_of(s * LANES, LANES), LANES)
                selected[half * held : (half + 1) * held, columns] = high
                selected[(2 + half) * held : (3 + half) * held, columns] = rest
            return carry

        lax.fori_loop(0, chips, select, 0)

    with jax.named_scope("dense"):
        loads[5].wait()

        def fill(a, carry):
            rows = pl.ds(pl.multiple_of(a * LANES, LANES), LANES)
            for b in range(blocks):
                dense[rows, b * LANES : (b + 1) * LANES] = tiles[place_s[0, a * blocks + b]]
            return carry

        lax.fori_loop(0, blocks, fill, 0)

    loads[6].wait()
    loads[7].wait()

    face_on = []
    for b in range(blocks):
        which = jnp.int32(6)
        for f in range(6):
            which = jnp.where(faces_s[0, f] == b, f, which)
        face_on.append(which)

    def sweep(k, carry):
        with jax.named_scope("wait_coarse"):
            waiter(coarse.at[k, pl.ds(0, peers)], coarse_sem.at[k]).wait_recv()
        with jax.named_scope("solve"):
            gathered = jnp.concatenate([coarse[k, s] for s in range(chips)], axis=1)
            both = dot_nt(gathered, selected[...])
            both = both[:, : 2 * held] + both[:, 2 * held :]
            mine = both[0:rights]
            if both.shape[0] > rights:
                mine = mine + both[rights:]
            partial[k, 0] = mine
            send(partial.at[k, 0], partial.at[k, 1], partial_sem.at[k], mate, j)
        with jax.named_scope("wait_mate"):
            waiter(partial.at[k, 1], partial_sem.at[k]).wait_recv()
        with jax.named_scope("send_solved"):
            solved[k, peers] = (mine + partial[k, 1]).astype(jnp.bfloat16)
            to_peers(solved.at[k, peers], solved.at[k], solved_sem.at[k])
            base = u_ref[...] + weights[...] * r_ref[...]
        with jax.named_scope("wait_solved"):
            waiter(solved.at[k, pl.ds(0, peers)], solved_sem.at[k]).wait_recv()
        with jax.named_scope("correct"):
            numbers = own_map[...]
            lane = numbers % LANES
            slot = (chip + chips - 1 - numbers // LANES) % chips
            own = jnp.zeros((rights, LANES), jnp.float32)
            for s in range(chips):
                own = jnp.where(slot == s, lanes_of(solved[k, s].astype(jnp.float32), lane), own)
            correction = lax.dot_general(
                own.astype(jnp.bfloat16), basis_t[...], (((1,), (0,)), ((), ())),
                preferred_element_type=jnp.float32,
            )
            u = base + correction
            u_ref[...] = u
            u_low = u.astype(jnp.bfloat16)
            for b in range(blocks):
                low[b] = u_low[:, b * LANES : (b + 1) * LANES]
        with jax.named_scope("send_faces"):
            for f in range(6):
                faces_out[k, f] = low[faces_s[0, f]]
            sems = face_sem.at[k]
            for f, by in ((1, 1), (0, regs - 1), (3, stride), (2, regs - stride)):
                send(faces_out.at[k, f], faces_in.at[k, f ^ 1], sems, i, (j + by) % regs)
            send(faces_out.at[k, 4], faces_in.at[k, 5], sems, before, j)
            send(faces_out.at[k, 5], faces_in.at[k, 4], sems, after, j)
        with jax.named_scope("local"):
            local = dot_nt(u_low, dense[...])
        with jax.named_scope("wait_faces"):
            waiter(faces_in.at[k], sems).wait_recv()
        with jax.named_scope("couple"):
            for f in range(6):
                permuted[f] = lanes_of(faces_in[k, f].astype(jnp.float32), match[f])
            coupling = jnp.concatenate([permuted[face_on[b]] for b in range(blocks)], axis=1)
            r_ref[...] = rhs[...] - (local - 0.5 * coupling)

        @pl.when(k < SWEEPS - 1)
        def _():
            with jax.named_scope("send_coarse"):
                send_coarse(k + 1)

        return carry

    lax.fori_loop(0, SWEEPS, sweep, 0)
    solution_o[...] = u_ref[...].astype(jnp.bfloat16)
    residual_o[...] = r_ref[...].astype(jnp.bfloat16)

    with jax.named_scope("all_sent"):
        waiter(inverse_h, inverse_sem).wait_send()
        waiter(ids.at[pl.ds(0, peers)], ids_sem).wait_send()
        for k in range(SWEEPS):
            waiter(coarse.at[k, pl.ds(0, peers)], coarse_sem.at[k]).wait_send()
            waiter(partial.at[k, 0], partial_sem.at[k]).wait_send()
            waiter(solved.at[k, pl.ds(0, peers)], solved_sem.at[k]).wait_send()
            waiter(faces_out.at[k], face_sem.at[k]).wait_send()


COARSE_ROWS = 2


def body(
    right_side,
    tiles,
    tile_list,
    weights,
    face_map,
    matching,
    coarse_basis,
    coarse_map,
    coarse_inverse,
):
    _, _, order, rights = right_side.shape
    listed, tile = tiles.shape[2:4]
    held, coarse_all = coarse_inverse.shape[1:]
    n_coarse = coarse_map.shape[2]
    subs, regs = lax.axis_size("sub"), lax.axis_size("reg")
    chips = subs // 2
    blocks = order // tile
    f32, bf16, i32 = jnp.float32, jnp.bfloat16, jnp.int32
    vmem = pltpu.VMEM
    dma = pltpu.SemaphoreType.DMA
    hbm = pl.BlockSpec(memory_space=pltpu.HBM)
    out = pl.BlockSpec(memory_space=pltpu.VMEM)
    results = pl.pallas_call(
        functools.partial(kernel, subs, regs),
        out_shape=[jax.ShapeDtypeStruct((rights, order), bf16)] * 2,
        in_specs=[hbm, hbm, hbm, hbm, pl.BlockSpec(memory_space=pltpu.SMEM), hbm, hbm, hbm, hbm],
        out_specs=[out, out],
        scratch_shapes=[
            vmem((rights, order), f32),
            vmem((listed + 1, tile, tile), bf16),
            vmem((2, listed), i32),
            vmem((1, order), f32),
            vmem((6, 1, tile), i32),
            vmem((order, n_coarse), bf16),
            vmem((n_coarse, order), bf16),
            vmem((1, n_coarse), i32),
            vmem((2, held, coarse_all), f32),
            vmem((order, order), bf16),
            vmem((4 * held, chips * n_coarse), bf16),
            vmem((1, LANES), i32),
            pltpu.SMEM((1, LANES), i32),
            vmem((chips, 1, n_coarse), i32),
            vmem((SWEEPS, chips, COARSE_ROWS * rights, n_coarse), bf16),
            vmem((SWEEPS, 2, rights, 2 * held), f32),
            vmem((SWEEPS, chips, rights, 2 * held), bf16),
            vmem((blocks, rights, tile), bf16),
            vmem((SWEEPS, 6, rights, tile), bf16),
            vmem((SWEEPS, 6, rights, tile), bf16),
            vmem((7, rights, tile), f32),
            vmem((rights, order), f32),
            vmem((rights, order), f32),
            dma((8,)),
            dma,
            dma((2,)),
            dma((2,)),
            dma((SWEEPS, 2)),
            dma((SWEEPS, 2)),
            dma((SWEEPS, 2)),
            dma((SWEEPS, 2)),
        ],
        compiler_params=pltpu.CompilerParams(
            collective_id=0, has_side_effects=True, vmem_limit_bytes=48 * 2**20
        ),
        cost_estimate=pl.CostEstimate(
            flops=SWEEPS * 2 * rights * order * (order + 2 * n_coarse),
            bytes_accessed=listed * tile * tile * 2 + held * coarse_all * 8,
            transcendentals=0,
        ),
        name="richardson",
    )(
        right_side[0, 0].T,
        tiles[0, 0],
        tile_list[0, 0].T,
        weights[0],
        face_map[0],
        matching.reshape(6, 1, tile),
        coarse_basis[0, 0],
        coarse_map[0],
        coarse_inverse[0],
    )
    return tuple(r.T.reshape(1, 1, order, rights) for r in results)


def solution(mesh):
    placed = (
        P("sub", "reg", None, None),
        P("sub", "reg", None, None, None),
        P("sub", "reg", None, None),
        P("sub", "reg", None),
        P("sub", "reg", None),
        P("sub", "reg", None, None),
        P("sub", "reg", None, None),
        P("sub", "reg", None),
        P("reg", "sub", None),
    )
    return jax.shard_map(
        body,
        mesh=mesh,
        in_specs=placed,
        out_specs=(P("sub", "reg", None, None), P("sub", "reg", None, None)),
        check_vma=False,
    )
```

time: 472 us -> 83.9 us (0.18)
  blocking collectives: 290 us -> 0 us
  starting transfers between devices: 79.5 us -> 0 us
  Pallas kernels: 0 us -> 73.6 us
  local copies, waits for them, and re-layouts: 66.4 us -> 9.23 us
  matrix products: 21.9 us -> 0 us
  other arithmetic: 4.82 us -> 0 us
    all_gather x7 -> x0, blocking collectives: 290 us -> none  [the longest x3 125 us: body(): lax.all_gather(local_coarse, 'sub', axis=0, tiled=True)]
    ppermute x18 -> x0, starting transfers between devices: 79.5 us -> none  [from_behind(): lax.ppermute(shard, axis, [(i, (i + by) % peers) for i in range(peers)])]
    pallas_call x0 -> x1, Pallas kernels: none -> 73.6 us  [body(): pl.pallas_call(functools.partial(kernel, subs, regs), out_shape=[jax.Shap...]
    gather x16 -> x0, local copies, waits for them, and re-layouts: 49.2 us -> none  [the longest x6 24.5 us: body(): permuted = jnp.take_along_axis(received, matched[:, :, None], axis=1)]
    dot_general x18 -> x0, matrix products: 21.9 us -> none  [the longest x3 8.63 us: body(): jnp.dot(selected, lax.all_gather(local_coarse, 'sub', axis=0, tiled=True)...]
    unnamed x68 -> x20, local copies, waits for them, and re-layouts: 13.9 us -> 9.23 us
  transfers between devices with their start and end apart: 18 -> 0, of which waited for: 2 -> 0; matrix products, arithmetic and copies ran while one was open for 4% -> 0% of each run, Pallas kernels for 0% -> 0%
where the time goes in v1:
time: 83.9 us; the launch traced here: 83.5 us
  Pallas kernels  73.6 us (88%)
  local copies, waits for them, and re-layouts  9.23 us (11%)
    pallas_call x1, Pallas kernels, body(): pl.pallas_call(functools.partial(kernel, subs, regs), out_shape=[jax.Shap...  73.6 us
    unnamed x20, local copies, waits for them, and re-layouts  9.23 us

profile of v1, /device:TPU:1, one launch (start us, length us, event | category | flops | bytes accessed | tf_op | source)
XLA Modules:
  0.0 83.5 jit_solution(7746828166437916891)
XLA Ops:
  0.6 0.0 copy-start
  0.6 1.7 %copy-done = bf16[1,1,80,128,128]{4,3,2,1,0:T(8,128)(2,1)S(1)} copy-done((bf16[1,1,80,128,128]{4,3,2,1,0:T(8,128)(2,1)S(1)}, bf16[1,1,80,128,128]{4,3,2,1,0:T(8,128)(2,1)}, u32[]{:S(2)}) %copy-start) | copy-done | bytes 2621464
  2.4 0.0 copy-start.1
  2.4 1.0 %copy-done.1 = f32[1,64,2048]{2,1,0:T(8,128)S(1)} copy-done((f32[1,64,2048]{2,1,0:T(8,128)S(1)}, f32[1,64,2048]{2,1,0:T(8,128)}, u32[]{:S(2)}) %copy-start.1) | copy-done | bytes 524312
  3.4 0.0 copy-start.2
  3.4 1.0 %copy-done.2 = bf16[1,1,1280,128]{3,2,1,0:T(8,128)(2,1)S(1)} copy-done((bf16[1,1,1280,128]{3,2,1,0:T(8,128)(2,1)S(1)}, bf16[1,1,1280,128]{3,2,1,0:T(8,128)(2,1)}, u32[]{:S(2)}) %copy-start.2) | copy-done | bytes 327704
  4.4 0.0 copy-start.3
  4.4 0.9 %copy-done.3 = f32[1,1,1280,16]{2,3,1,0:T(8,128)S(1)} copy-done((f32[1,1,1280,16]{2,3,1,0:T(8,128)S(1)}, f32[1,1,1280,16]{2,3,1,0:T(8,128)}, u32[]{:S(2)}) %copy-start.3) | copy-done | bytes 81944
  5.3 0.0 copy-start.4
  5.3 0.7 copy-done.4
  6.0 0.0 copy-start.5
  6.0 0.7 copy-done.5
  6.7 0.0 copy-start.6
  6.7 0.7 copy-done.6
  7.3 0.0 copy-start.7
  7.3 0.7 copy-done.7
  8.0 0.0 copy-start.8
  8.0 0.7 copy-done.8
  8.6 73.6 %richardson.1 = (bf16[16,1280]{1,0:T(8,128)(2,1)S(1)}, bf16[16,1280]{1,0:T(8,128)(2,1)S(1)}) custom-call(f32[16,1280]{1,0:T(8,128)S(1)} %bitcast.22, bf16[80,128,128]{2,1,0:T(8,128)(2,1)S(1)} %bitcast.19, s32[2,80]{1,0:T(2,128)S(1)} %bitcast.27, f32[1,1280]{1,0:T(1,128)S(1)} %bitcast.25, s32[1,6]{1,0:T(1,128)S(1)} %bitcast.28, s32[6,1,128]{2,1,0:T(1,128)S(1)} %bitcast.26, ...), custom_call_target="tpu_custom_call" | custom-call | flops 188743680 | bytes 3670016 | tf_op jit(solution)/shard_map/richardson/pallas_call | solution.py:322
  82.3 0.6 copy.13
  82.9 0.6 copy.14
Async XLA Ops:
  0.6 1.7 %copy-start = (bf16[1,1,80,128,128]{4,3,2,1,0:T(8,128)(2,1)S(1)}, bf16[1,1,80,128,128]{4,3,2,1,0:T(8,128)(2,1)}, u32[]{:S(2)}) copy-start(bf16[1,1,80,128,128]{4,3,2,1,0:T(8,128)(2,1)} %param.10) | copy-start | bytes 7864324
  2.4 1.0 %copy-start.1 = (f32[1,64,2048]{2,1,0:T(8,128)S(1)}, f32[1,64,2048]{2,1,0:T(8,128)}, u32[]{:S(2)}) copy-start(f32[1,64,2048]{2,1,0:T(8,128)} %param.17) | copy-start | bytes 1572868
  3.4 1.0 %copy-start.2 = (bf16[1,1,1280,128]{3,2,1,0:T(8,128)(2,1)S(1)}, bf16[1,1,1280,128]{3,2,1,0:T(8,128)(2,1)}, u32[]{:S(2)}) copy-start(bf16[1,1,1280,128]{3,2,1,0:T(8,128)(2,1)} %param.15) | copy-start | bytes 983044
  4.4 0.9 %copy-start.3 = (f32[1,1,1280,16]{2,3,1,0:T(8,128)S(1)}, f32[1,1,1280,16]{2,3,1,0:T(8,128)}, u32[]{:S(2)}) copy-start(f32[1,1,1280,16]{2,3,1,0:T(8,128)} %param.9) | copy-start | bytes 245764
  5.3 0.7 copy-start.4
  6.0 0.7 copy-start.5
  6.7 0.7 copy-start.6
  7.3 0.7 copy-start.7
  8.0 0.7 copy-start.8

commit v2 on v1

v2 whole, which is shorter than its diff:
```python
import functools

import jax
import jax.numpy as jnp
from jax import lax
from jax.experimental import pallas as pl
from jax.experimental.pallas import tpu as pltpu
from jax.sharding import PartitionSpec as P

SWEEPS = 3
MESH = pl.DeviceIdType.MESH
LANES = 128
GROUP = 4


def dot_nt(a, b):
    return lax.dot_general(a, b, (((1,), (1,)), ((), ())), preferred_element_type=jnp.float32)


def lanes_of(x, ids):
    ids = jnp.broadcast_to(ids, x.shape)
    return jnp.take_along_axis(x, ids, axis=1, mode="promise_in_bounds")


def split(x):
    high = x.astype(jnp.bfloat16)
    return high, (x - high.astype(jnp.float32)).astype(jnp.bfloat16)


def kernel(
    subs,
    regs,
    rhs_h,
    tiles_h,
    list_h,
    weights_h,
    faces_s,
    match_h,
    basis_h,
    map_h,
    inverse_h,
    result_o,
    rhs,
    tiles,
    listing,
    weights,
    match,
    basis,
    basis_t,
    own_map,
    inverse,
    halves,
    dense,
    selected,
    place,
    place_s,
    ids,
    coarse,
    partial,
    solved,
    low,
    faces_out,
    faces_in,
    permuted,
    u_ref,
    r_ref,
    local_sem,
    place_sem,
    inverse_sem,
    ids_sem,
    coarse_sem,
    partial_sem,
    solved_sem,
    face_sem,
):
    rights, order = rhs.shape
    blocks = order // LANES
    listed = tiles_h.shape[0]
    held = inverse_h.shape[0]
    chips = subs // 2
    groups = chips // GROUP
    stride = max(regs // 4, 1)
    i, j = lax.axis_index("sub"), lax.axis_index("reg")
    core = i % 2
    x, z = (i // 2) % GROUP, i // (2 * GROUP)
    mate = i + 1 - 2 * core
    after, before = (i + 1) % subs, (i + subs - 1) % subs
    apart = (i + subs - 1 + 2 * core) % subs

    far = (
        jnp.where(z == 0, 3, jnp.where(z == 3, 1, 2)),
        jnp.where(z == 0, 2, jnp.where(z == 3, 2, 3)),
        jnp.where(z == 0, 1, jnp.where(z == 3, 3, 1)),
    )

    def pick(n, options):
        which = options[-1]
        for m in range(len(options) - 1):
            which = jnp.where(n == m, options[m], which)
        return which

    def peer(a, b):
        return (((z + a) % groups) * GROUP + (x + b) % GROUP) * 2 + core

    def send(src, dst, sems, to_sub, to_reg):
        pltpu.make_async_remote_copy(
            src_ref=src, dst_ref=dst, send_sem=sems.at[0], recv_sem=sems.at[1],
            device_id=(to_sub, to_reg), device_id_type=MESH,
        ).start()

    def waiter(ref, sems):
        return pltpu.make_async_remote_copy(
            src_ref=ref, dst_ref=ref, send_sem=sems.at[0], recv_sem=sems.at[1],
            device_id=(mate, j), device_id_type=MESH,
        )

    loads = [
        (map_h, own_map),
        (basis_h, basis),
        (rhs_h, rhs),
        (inverse_h, inverse.at[core]),
        (list_h, listing),
        (tiles_h, tiles.at[pl.ds(0, listed)]),
        (weights_h, weights),
        (match_h, match),
    ]
    loads = [pltpu.make_async_copy(a, b, local_sem.at[n]) for n, (a, b) in enumerate(loads)]
    for load in loads:
        load.start()

    barrier = pltpu.get_barrier_semaphore()

    def greet(to_sub, to_reg):
        pl.semaphore_signal(barrier, inc=1, device_id=(to_sub, to_reg), device_id_type=MESH)

    def each_peer(act):
        def one(n, carry):
            act(pick(n // GROUP, (*far, 0)), pick(n % GROUP, (2, 1, 3, 0)))
            return carry

        lax.fori_loop(0, chips - 1, one, 0)

    for by in (1, regs - 1, stride, regs - stride):
        greet(i, (j + by) % regs)
    each_peer(lambda a, b: greet(peer(a, b), j))
    greet(mate, j)
    greet(apart, j)

    def to_peers(box, sems):
        def act(a, b):
            send(box.at[0], box.at[a * GROUP + b], sems.at[a], peer(a, b), j)

        each_peer(act)

    def arrived(box, sems, a):
        waiter(box.at[pl.ds(a * GROUP, GROUP)], sems.at[a]).wait_recv()

    def arrived_near(box, sems):
        waiter(box.at[pl.ds(1, GROUP - 1)], sems.at[0]).wait_recv()

    def sent(box, sems):
        waiter(box.at[pl.ds(1, GROUP - 1)], sems.at[0]).wait_send()
        for a in range(1, groups):
            waiter(box.at[pl.ds(a * GROUP, GROUP)], sems.at[a]).wait_send()

    def near_to_far(box, sems, act):
        arrived_near(box, sems)
        act(0)
        for a in far[::-1]:
            arrived(box, sems, a)
            act(a)

    def make_coarse(k):
        now = lax.dot_general(
            r_ref[...].astype(jnp.bfloat16), basis[...], (((1,), (0,)), ((), ())),
            preferred_element_type=jnp.float32,
        )
        high, rest = split(now)
        coarse[k, 0, 0:rights] = high
        coarse[k, 0, rights:] = rest

    loads[1].wait()
    loads[2].wait()
    r_ref[...] = rhs[...]
    u_ref[...] = jnp.zeros_like(u_ref)
    make_coarse(0)
    loads[0].wait()
    ids[0] = own_map[...]

    pl.semaphore_wait(barrier, chips + 5)
    to_peers(ids, ids_sem)
    send(inverse_h, inverse.at[core], inverse_sem, mate, j)
    to_peers(coarse.at[0], coarse_sem.at[0])

    tiles[listed] = jnp.zeros_like(tiles[listed])
    permuted[6] = jnp.zeros_like(permuted[6])
    loads[4].wait()
    pair = listing[0:1, :] * blocks + listing[1:2, :]
    shape = (LANES, listed)
    hit = lax.broadcasted_iota(jnp.int32, shape, 0) == jnp.broadcast_to(pair, shape)
    number = lax.broadcasted_iota(jnp.int32, shape, 1)
    found = jnp.min(jnp.where(hit, number, listed), axis=1, keepdims=True)
    place[...] = jnp.broadcast_to(found, (LANES, LANES)).T[0:1]
    to_scalars = pltpu.make_async_copy(place, place_s, place_sem)
    to_scalars.start()

    def keep_split(half):
        high, rest = split(inverse[half])
        rows = pl.ds(pl.multiple_of(half * held, held), held)
        halves[rows, :] = high
        rows = pl.ds(pl.multiple_of((2 + half) * held, held), held)
        halves[rows, :] = rest

    loads[3].wait()
    keep_split(core)
    waiter(inverse.at[1 - core], inverse_sem).wait_recv()
    keep_split(1 - core)

    def select(a):
        for t in range(0, GROUP, 2):
            numbers = jnp.concatenate([ids[a * GROUP + t], ids[a * GROUP + t + 1]], axis=1)
            lane, block = numbers & (LANES - 1), numbers >> 7
            shape = (LANES, 2 * LANES)
            at_lane = lax.broadcasted_iota(jnp.int32, shape, 0) == jnp.broadcast_to(lane, shape)
            at_lane = jnp.where(at_lane, 1.0, 0.0).astype(jnp.bfloat16)
            picks = []
            for b in range(chips):
                at_block = jnp.where(block == b, 1.0, 0.0).astype(jnp.bfloat16)
                picks.append(at_lane * jnp.broadcast_to(at_block, shape))
            chosen = jnp.dot(
                halves[...], jnp.concatenate(picks, axis=0), preferred_element_type=jnp.float32
            )
            selected[a, :, t * LANES : (t + 2) * LANES] = chosen.astype(jnp.bfloat16)

    near_to_far(ids, ids_sem, select)

    for b in range(blocks):
        basis_t[:, b * LANES : (b + 1) * LANES] = basis[b * LANES : (b + 1) * LANES, :].T
    to_scalars.wait()
    loads[5].wait()

    def fill(a, carry):
        rows = pl.ds(pl.multiple_of(a * LANES, LANES), LANES)
        for b in range(blocks):
            dense[rows, b * LANES : (b + 1) * LANES] = tiles[place_s[0, a * blocks + b]]
        return carry

    lax.fori_loop(0, blocks, fill, 0)
    loads[6].wait()
    loads[7].wait()

    face_on = []
    for b in range(blocks):
        which = jnp.int32(6)
        for f in range(6):
            which = jnp.where(faces_s[0, f] == b, f, which)
        face_on.append(which)

    def sweep(k, carry):
        totals = []

        def solve(a):
            gathered = jnp.concatenate([coarse[k, a * GROUP + t] for t in range(GROUP)], axis=1)
            totals.append(dot_nt(gathered, selected[a]))

        near_to_far(coarse.at[k], coarse_sem.at[k], solve)
        both = (totals[0] + totals[1]) + (totals[2] + totals[3])
        both = both[:, : 2 * held] + both[:, 2 * held :]
        mine = both[0:rights] + both[rights:]
        partial[k, 0] = mine
        send(partial.at[k, 0], partial.at[k, 1], partial_sem.at[k], mate, j)
        base = u_ref[...] + weights[...] * r_ref[...]
        waiter(partial.at[k, 1], partial_sem.at[k]).wait_recv()
        solved[k, 0] = (mine + partial[k, 1]).astype(jnp.bfloat16)
        to_peers(solved.at[k], solved_sem.at[k])

        numbers = own_map[...]
        lane, chip = numbers & (LANES - 1), numbers >> 7
        slot = ((z + groups - (chip >> 2)) & 3) * GROUP + ((x + GROUP - (chip & 3)) & 3)
        found = [jnp.zeros((rights, LANES), jnp.float32)]

        def collect(a):
            own = found[-1]
            for t in range(GROUP):
                here = lanes_of(solved[k, a * GROUP + t].astype(jnp.float32), lane)
                own = jnp.where(slot == a * GROUP + t, here, own)
            found.append(own)

        near_to_far(solved.at[k], solved_sem.at[k], collect)
        correction = lax.dot_general(
            found[-1].astype(jnp.bfloat16), basis_t[...], (((1,), (0,)), ((), ())),
            preferred_element_type=jnp.float32,
        )
        u = base + correction
        u_ref[...] = u
        u_low = u.astype(jnp.bfloat16)
        for b in range(blocks):
            low[b] = u_low[:, b * LANES : (b + 1) * LANES]
        for f in range(6):
            faces_out[k, f] = low[faces_s[0, f]]
        sems = face_sem.at[k]
        for f, by in ((1, 1), (0, regs - 1), (3, stride), (2, regs - stride)):
            send(faces_out.at[k, f], faces_in.at[k, f ^ 1], sems, i, (j + by) % regs)
        send(faces_out.at[k, 4], faces_in.at[k, 5], sems, before, j)
        send(faces_out.at[k, 5], faces_in.at[k, 4], sems, after, j)
        local = dot_nt(u_low, dense[...])
        waiter(faces_in.at[k], sems).wait_recv()
        for f in range(6):
            permuted[f] = lanes_of(faces_in[k, f].astype(jnp.float32), match[f])
        coupling = jnp.concatenate([permuted[face_on[b]] for b in range(blocks)], axis=1)
        r_ref[...] = rhs[...] - (local - 0.5 * coupling)

        @pl.when(k < SWEEPS - 1)
        def _():
            make_coarse(k + 1)
            to_peers(coarse.at[k + 1], coarse_sem.at[k + 1])

        return carry

    lax.fori_loop(0, SWEEPS, sweep, 0)
    result_o[0] = u_ref[...].astype(result_o.dtype)
    result_o[1] = r_ref[...].astype(result_o.dtype)

    waiter(inverse_h, inverse_sem).wait_send()
    sent(ids, ids_sem)
    for k in range(SWEEPS):
        sent(coarse.at[k], coarse_sem.at[k])
        waiter(partial.at[k, 0], partial_sem.at[k]).wait_send()
        sent(solved.at[k], solved_sem.at[k])
        waiter(faces_out.at[k], face_sem.at[k]).wait_send()


def body(
    right_side,
    tiles,
    tile_list,
    weights,
    face_map,
    matching,
    coarse_basis,
    coarse_map,
    coarse_inverse,
):
    _, _, order, rights = right_side.shape
    listed, tile = tiles.shape[2:4]
    held, coarse_all = coarse_inverse.shape[1:]
    n_coarse = coarse_map.shape[2]
    subs, regs = lax.axis_size("sub"), lax.axis_size("reg")
    chips = subs // 2
    blocks = order // tile
    f32, bf16, i32 = jnp.float32, jnp.bfloat16, jnp.int32
    vmem = pltpu.VMEM
    dma = pltpu.SemaphoreType.DMA
    hbm = pl.BlockSpec(memory_space=pltpu.HBM)
    result = pl.pallas_call(
        functools.partial(kernel, subs, regs),
        out_shape=jax.ShapeDtypeStruct((2, rights, order), bf16),
        in_specs=[hbm, hbm, hbm, hbm, pl.BlockSpec(memory_space=pltpu.SMEM), hbm, hbm, hbm, hbm],
        out_specs=pl.BlockSpec(memory_space=pltpu.VMEM),
        scratch_shapes=[
            vmem((rights, order), f32),
            vmem((listed + 1, tile, tile), bf16),
            vmem((2, listed), i32),
            vmem((1, order), f32),
            vmem((6, 1, tile), i32),
            vmem((order, n_coarse), bf16),
            vmem((n_coarse, order), bf16),
            vmem((1, n_coarse), i32),
            vmem((2, held, coarse_all), f32),
            vmem((4 * held, coarse_all), bf16),
            vmem((order, order), bf16),
            vmem((chips // GROUP, 4 * held, GROUP * n_coarse), bf16),
            vmem((1, LANES), i32),
            pltpu.SMEM((1, LANES), i32),
            vmem((chips, 1, n_coarse), i32),
            vmem((SWEEPS, chips, 2 * rights, n_coarse), bf16),
            vmem((SWEEPS, 2, rights, 2 * held), f32),
            vmem((SWEEPS, chips, rights, 2 * held), bf16),
            vmem((blocks, rights, tile), bf16),
            vmem((SWEEPS, 6, rights, tile), bf16),
            vmem((SWEEPS, 6, rights, tile), bf16),
            vmem((7, rights, tile), f32),
            vmem((rights, order), f32),
            vmem((rights, order), f32),
            dma((8,)),
            dma,
            dma((2,)),
            dma((GROUP, 2)),
            dma((SWEEPS, GROUP, 2)),
            dma((SWEEPS, 2)),
            dma((SWEEPS, GROUP, 2)),
            dma((SWEEPS, 2)),
        ],
        compiler_params=pltpu.CompilerParams(
            collective_id=0, has_side_effects=True, vmem_limit_bytes=56 * 2**20
        ),
        cost_estimate=pl.CostEstimate(
            flops=SWEEPS * 2 * rights * order * (order + 2 * n_coarse),
            bytes_accessed=listed * tile * tile * 2 + held * coarse_all * 8,
            transcendentals=0,
        ),
        name="richardson",
    )(
        right_side[0, 0].T,
        tiles[0, 0],
        tile_list[0, 0].T,
        weights[0],
        face_map[0],
        matching.reshape(6, 1, tile),
        coarse_basis[0, 0],
        coarse_map[0],
        coarse_inverse[0],
    )
    return tuple(result[n].T.reshape(1, 1, order, rights).astype(bf16) for n in range(2))


def solution(mesh):
    placed = (
        P("sub", "reg", None, None),
        P("sub", "reg", None, None, None),
        P("sub", "reg", None, None),
        P("sub", "reg", None),
        P("sub", "reg", None),
        P("sub", "reg", None, None),
        P("sub", "reg", None, None),
        P("sub", "reg", None),
        P("reg", "sub", None),
    )
    return jax.shard_map(
        body,
        mesh=mesh,
        in_specs=placed,
        out_specs=(P("sub", "reg", None, None), P("sub", "reg", None, None)),
        check_vma=False,
    )
```

time: 83.9 us -> 72.2 us (0.86)
  local copies, waits for them, and re-layouts: 9.23 us -> 1.43 us
  Pallas kernels: 73.6 us -> 70 us
    unnamed x20 -> x0, local copies, waits for them, and re-layouts: 9.23 us -> none
    pallas_call x1, Pallas kernels: 73.6 us -> 70 us  [body(): pl.pallas_call(functools.partial(kernel, subs, regs), out_shape=jax.Shape...]
    reshape x0 -> x1, local copies, waits for them, and re-layouts: none -> 1.43 us  [body(): result[n].T.reshape(1, 1, order, rights).astype(bf16)]
where the time goes in v2:
time: 72.2 us; the launch traced here: 72 us
  Pallas kernels  70 us (97%)
  local copies, waits for them, and re-layouts  1.43 us (2%)
    pallas_call x1, Pallas kernels, body(): pl.pallas_call(functools.partial(kernel, subs, regs), out_shape=jax.Shape...  70 us

profile of v2, /device:TPU:1, one launch (start us, length us, event | category | flops | bytes accessed | tf_op | source)
XLA Modules:
  0.0 72.0 jit_solution(15334741360066409782)
XLA Ops:
  0.6 70.0 %richardson.1 = bf16[2,16,1280]{2,1,0:T(8,128)(2,1)} custom-call(f32[16,1280]{1,0:T(8,128)} %bitcast.28, bf16[80,128,128]{2,1,0:T(8,128)(2,1)} %bitcast.25, s32[2,80]{1,0:T(2,128)} %bitcast.31, f32[1,1280]{1,0:T(1,128)} %bitcast.29, s32[1,6]{1,0:T(1,128)} %bitcast.32, s32[6,1,128]{2,1,0:T(1,128)} %bitcast.30, bf16[1280,128]{1,0:T(8,128)(2,1)} %bitcast.27, ...), custom_call_target="tpu_custom_call" | custom-call | flops 188743680 | bytes 3670016 | tf_op jit(solution)/shard_map/richardson/pallas_call | solution.py:355
  70.6 1.4 %slice_bitcast_fusion = (bf16[1,1,1280,16]{2,3,1,0:T(8,128)(2,1)}, bf16[1,1,1280,16]{2,3,1,0:T(8,128)(2,1)}) fusion(bf16[2,16,1280]{2,1,0:T(8,128)(2,1)} %richardson.1), kind=kLoop, calls=%fused_computation | loop fusion | bytes 163840 | tf_op jit(solution)/shard_map/reshape | solution.py:414

commit v3 on v2

--- a/solution.py
+++ b/solution.py
@@ -15,6 +15,10 @@
 
 def dot_nt(a, b):
     return lax.dot_general(a, b, (((1,), (1,)), ((), ())), preferred_element_type=jnp.float32)
+
+
+def dot(a, b):
+    return jnp.dot(a, b, preferred_element_type=jnp.float32)
 
 
 def lanes_of(x, ids):
@@ -34,7 +38,7 @@
     tiles_h,
     list_h,
     weights_h,
-    faces_s,
+    faces_h,
     match_h,
     basis_h,
     map_h,
@@ -47,6 +51,9 @@
     match,
     basis,
     basis_t,
+    face_basis,
+    face_basis_t,
+    faces_s,
     own_map,
     inverse,
     halves,
@@ -58,7 +65,7 @@
     coarse,
     partial,
     solved,
-    low,
+    by_block,
     faces_out,
     faces_in,
     permuted,
@@ -77,6 +84,7 @@
     blocks = order // LANES
     listed = tiles_h.shape[0]
     held = inverse_h.shape[0]
+    n_coarse = basis.shape[2]
     chips = subs // 2
     groups = chips // GROUP
     stride = max(regs // 4, 1)
@@ -84,6 +92,7 @@
     core = i % 2
     x, z = (i // 2) % GROUP, i // (2 * GROUP)
     mate = i + 1 - 2 * core
+    y = j % stride
     after, before = (i + 1) % subs, (i + subs - 1) % subs
     apart = (i + subs - 1 + 2 * core) % subs
 
@@ -123,6 +132,7 @@
         (tiles_h, tiles.at[pl.ds(0, listed)]),
         (weights_h, weights),
         (match_h, match),
+        (faces_h, faces_s),
     ]
     loads = [pltpu.make_async_copy(a, b, local_sem.at[n]) for n, (a, b) in enumerate(loads)]
     for load in loads:
@@ -170,20 +180,19 @@
             arrived(box, sems, a)
             act(a)
 
-    def make_coarse(k):
-        now = lax.dot_general(
-            r_ref[...].astype(jnp.bfloat16), basis[...], (((1,), (0,)), ((), ())),
-            preferred_element_type=jnp.float32,
-        )
+    def keep_coarse(k, now):
         high, rest = split(now)
         coarse[k, 0, 0:rights] = high
         coarse[k, 0, rights:] = rest
+
+    def on_basis(r):
+        return dot(r.astype(jnp.bfloat16), basis[...].reshape(order, n_coarse))
 
     loads[1].wait()
     loads[2].wait()
     r_ref[...] = rhs[...]
     u_ref[...] = jnp.zeros_like(u_ref)
-    make_coarse(0)
+    keep_coarse(0, on_basis(rhs[...]))
     loads[0].wait()
     ids[0] = own_map[...]
 
@@ -210,6 +219,33 @@
         halves[rows, :] = high
         rows = pl.ds(pl.multiple_of((2 + half) * held, held), held)
         halves[rows, :] = rest
+
+    loads[8].wait()
+    face_on = []
+    for b in range(blocks):
+        which = jnp.int32(6)
+        for f in range(6):
+            which = jnp.where(faces_s[0, f] == b, f, which)
+        face_on.append(which)
+    for f in range(6):
+        lanes = slice(f * LANES, (f + 1) * LANES)
+        block = basis[faces_s[0, f]]
+        face_basis[lanes] = block
+        face_basis_t[:, lanes] = block.T
+    for b in range(blocks):
+        basis_t[:, b * LANES : (b + 1) * LANES] = basis[b].T
+    to_scalars.wait()
+    loads[5].wait()
+
+    def fill(a, carry):
+        rows = pl.ds(pl.multiple_of(a * LANES, LANES), LANES)
+        for b in range(blocks):
+            dense[rows, b * LANES : (b + 1) * LANES] = tiles[place_s[0, a * blocks + b]]
+        return carry
+
+    lax.fori_loop(0, blocks, fill, 0)
+    loads[6].wait()
+    loads[7].wait()
 
     loads[3].wait()
     keep_split(core)
@@ -233,28 +269,13 @@
             selected[a, :, t * LANES : (t + 2) * LANES] = chosen.astype(jnp.bfloat16)
 
     near_to_far(ids, ids_sem, select)
-
-    for b in range(blocks):
-        basis_t[:, b * LANES : (b + 1) * LANES] = basis[b * LANES : (b + 1) * LANES, :].T
-    to_scalars.wait()
-    loads[5].wait()
-
-    def fill(a, carry):
-        rows = pl.ds(pl.multiple_of(a * LANES, LANES), LANES)
+    waiter(inverse_h, inverse_sem).wait_send()
+    sent(ids, ids_sem)
+
+    def faces_of(field):
         for b in range(blocks):
-            dense[rows, b * LANES : (b + 1) * LANES] = tiles[place_s[0, a * blocks + b]]
-        return carry
-
-    lax.fori_loop(0, blocks, fill, 0)
-    loads[6].wait()
-    loads[7].wait()
-
-    face_on = []
-    for b in range(blocks):
-        which = jnp.int32(6)
-        for f in range(6):
-            which = jnp.where(faces_s[0, f] == b, f, which)
-        face_on.append(which)
+            by_block[b] = field[:, b * LANES : (b + 1) * LANES]
+        return jnp.concatenate([by_block[faces_s[0, f]] for f in range(6)], axis=1)
 
     def sweep(k, carry):
         totals = []
@@ -270,6 +291,7 @@
         partial[k, 0] = mine
         send(partial.at[k, 0], partial.at[k, 1], partial_sem.at[k], mate, j)
         base = u_ref[...] + weights[...] * r_ref[...]
+        base_faces = faces_of(base)
         waiter(partial.at[k, 1], partial_sem.at[k]).wait_recv()
         solved[k, 0] = (mine + partial[k, 1]).astype(jnp.bfloat16)
         to_peers(solved.at[k], solved_sem.at[k])
@@ -287,46 +309,53 @@
             found.append(own)
 
         near_to_far(solved.at[k], solved_sem.at[k], collect)
-        correction = lax.dot_general(
-            found[-1].astype(jnp.bfloat16), basis_t[...], (((1,), (0,)), ((), ())),
-            preferred_element_type=jnp.float32,
-        )
-        u = base + correction
-        u_ref[...] = u
-        u_low = u.astype(jnp.bfloat16)
-        for b in range(blocks):
-            low[b] = u_low[:, b * LANES : (b + 1) * LANES]
+        own = found[-1].astype(jnp.bfloat16)
+        u_faces = (base_faces + dot(own, face_basis_t[...])).astype(jnp.bfloat16)
         for f in range(6):
-            faces_out[k, f] = low[faces_s[0, f]]
+            faces_out[k, f] = u_faces[:, f * LANES : (f + 1) * LANES]
         sems = face_sem.at[k]
-        for f, by in ((1, 1), (0, regs - 1), (3, stride), (2, regs - stride)):
-            send(faces_out.at[k, f], faces_in.at[k, f ^ 1], sems, i, (j + by) % regs)
+
+        def send_face(n, carry):
+            f = pick(n, (pick(y, (0, 3, 3, 1)), pick(y, (3, 2, 2, 3)), pick(y, (2, 1, 1, 2)), pick(y, (1, 0, 0, 0))))
+            by = pick(f, (regs - 1, 1, regs - stride, stride))
+            send(faces_out.at[k, f], faces_in.at[k, f + 1 - 2 * (f % 2)], sems, i, (j + by) % regs)
+            return carry
+
+        lax.fori_loop(0, 4, send_face, 0)
         send(faces_out.at[k, 4], faces_in.at[k, 5], sems, before, j)
         send(faces_out.at[k, 5], faces_in.at[k, 4], sems, after, j)
-        local = dot_nt(u_low, dense[...])
+
+        u = base + dot(own, basis_t[...])
+        u_ref[...] = u
+        here = rhs[...] - dot_nt(u.astype(jnp.bfloat16), dense[...])
+        here_faces = faces_of(here)
+        inside = [
+            jnp.where(face_on[b] == 6, here[:, b * LANES : (b + 1) * LANES], 0.0) for b in range(blocks)
+        ]
+        coarse_inside = on_basis(jnp.concatenate(inside, axis=1))
+        sent(coarse.at[k], coarse_sem.at[k])
+        waiter(partial.at[k, 0], partial_sem.at[k]).wait_send()
+        sent(solved.at[k], solved_sem.at[k])
+
         waiter(faces_in.at[k], sems).wait_recv()
-        for f in range(6):
-            permuted[f] = lanes_of(faces_in[k, f].astype(jnp.float32), match[f])
-        coupling = jnp.concatenate([permuted[face_on[b]] for b in range(blocks)], axis=1)
-        r_ref[...] = rhs[...] - (local - 0.5 * coupling)
+        coupling = [0.5 * lanes_of(faces_in[k, f].astype(jnp.float32), match[f]) for f in range(6)]
 
         @pl.when(k < SWEEPS - 1)
         def _():
-            make_coarse(k + 1)
+            r_faces = here_faces + jnp.concatenate(coupling, axis=1)
+            keep_coarse(k + 1, coarse_inside + dot(r_faces.astype(jnp.bfloat16), face_basis[...]))
             to_peers(coarse.at[k + 1], coarse_sem.at[k + 1])
 
+        for f in range(6):
+            permuted[f] = coupling[f]
+        r_ref[...] = here + jnp.concatenate([permuted[face_on[b]] for b in range(blocks)], axis=1)
         return carry
 
     lax.fori_loop(0, SWEEPS, sweep, 0)
     result_o[0] = u_ref[...].astype(result_o.dtype)
     result_o[1] = r_ref[...].astype(result_o.dtype)
 
-    waiter(inverse_h, inverse_sem).wait_send()
-    sent(ids, ids_sem)
     for k in range(SWEEPS):
-        sent(coarse.at[k], coarse_sem.at[k])
-        waiter(partial.at[k, 0], partial_sem.at[k]).wait_send()
-        sent(solved.at[k], solved_sem.at[k])
         waiter(faces_out.at[k], face_sem.at[k]).wait_send()
 
 
@@ -354,8 +383,8 @@
     hbm = pl.BlockSpec(memory_space=pltpu.HBM)
     result = pl.pallas_call(
         functools.partial(kernel, subs, regs),
-        out_shape=jax.ShapeDtypeStruct((2, rights, order), bf16),
-        in_specs=[hbm, hbm, hbm, hbm, pl.BlockSpec(memory_space=pltpu.SMEM), hbm, hbm, hbm, hbm],
+        out_shape=pltpu.VMEM((2, rights, order), bf16),
+        in_specs=[hbm] * 9,
         out_specs=pl.BlockSpec(memory_space=pltpu.VMEM),
         scratch_shapes=[
             vmem((rights, order), f32),
@@ -363,8 +392,11 @@
             vmem((2, listed), i32),
             vmem((1, order), f32),
             vmem((6, 1, tile), i32),
-            vmem((order, n_coarse), bf16),
+            vmem((blocks, tile, n_coarse), bf16),
             vmem((n_coarse, order), bf16),
+            vmem((6 * tile, n_coarse), bf16),
+            vmem((n_coarse, 6 * tile), bf16),
+            pltpu.SMEM((1, 6), i32),
             vmem((1, n_coarse), i32),
             vmem((2, held, coarse_all), f32),
             vmem((4 * held, coarse_all), bf16),
@@ -376,13 +408,13 @@
             vmem((SWEEPS, chips, 2 * rights, n_coarse), bf16),
             vmem((SWEEPS, 2, rights, 2 * held), f32),
             vmem((SWEEPS, chips, rights, 2 * held), bf16),
-            vmem((blocks, rights, tile), bf16),
+            vmem((blocks, rights, tile), f32),
             vmem((SWEEPS, 6, rights, tile), bf16),
             vmem((SWEEPS, 6, rights, tile), bf16),
             vmem((7, rights, tile), f32),
             vmem((rights, order), f32),
             vmem((rights, order), f32),
-            dma((8,)),
+            dma((9,)),
             dma,
             dma((2,)),
             dma((GROUP, 2)),
@@ -407,7 +439,7 @@
         weights[0],
         face_map[0],
         matching.reshape(6, 1, tile),
-        coarse_basis[0, 0],
+        coarse_basis.reshape(blocks, tile, n_coarse),
         coarse_map[0],
         coarse_inverse[0],
     )

time: 72.2 us -> 69 us (0.956)
  Pallas kernels: 70 us -> 67.6 us
  local copies, waits for them, and re-layouts: 1.43 us -> 0.64 us
    pallas_call x1, Pallas kernels: 70 us -> 67.6 us  [body(): pl.pallas_call(functools.partial(kernel, subs, regs), out_shape=pltpu.VME...]
    reshape x1, local copies, waits for them, and re-layouts: 1.43 us -> 0.64 us  [body(): result[n].T.reshape(1, 1, order, rights).astype(bf16)]
where the time goes in v3:
time: 69 us; the launch traced here: 68.9 us
  Pallas kernels  67.6 us (98%)
    pallas_call x1, Pallas kernels, body(): pl.pallas_call(functools.partial(kernel, subs, regs), out_shape=pltpu.VME...  67.6 us

profile of v3, /device:TPU:1, one launch (start us, length us, event | category | flops | bytes accessed | tf_op | source)
XLA Modules:
  0.0 68.9 jit_solution(10782783677153318596)
XLA Ops:
  0.6 67.6 %richardson.1 = bf16[2,16,1280]{2,1,0:T(8,128)(2,1)S(1)} custom-call(f32[16,1280]{1,0:T(8,128)} %bitcast.28, bf16[80,128,128]{2,1,0:T(8,128)(2,1)} %bitcast.25, s32[2,80]{1,0:T(2,128)} %bitcast.31, f32[1,1280]{1,0:T(1,128)} %bitcast.29, s32[1,6]{1,0:T(1,128)} %bitcast.32, s32[6,1,128]{2,1,0:T(1,128)} %bitcast.30, bf16[10,128,128]{2,1,0:T(8,128)(2,1)} %bitcast.27, ...), custom_call_target="tpu_custom_call" | custom-call | flops 188743680 | bytes 3670016 | tf_op jit(solution)/shard_map/richardson/pallas_call | solution.py:384
  68.3 0.6 slice_bitcast_fusion

commit v4 on v3

--- a/solution.py
+++ b/solution.py
@@ -156,9 +156,9 @@
     greet(mate, j)
     greet(apart, j)
 
-    def to_peers(box, sems):
+    def to_peers(box, sems, grouped=False):
         def act(a, b):
-            send(box.at[0], box.at[a * GROUP + b], sems.at[a], peer(a, b), j)
+            send(box.at[0], box.at[a * GROUP + b], sems.at[a] if grouped else sems, peer(a, b), j)
 
         each_peer(act)
 
@@ -188,18 +188,17 @@
     def on_basis(r):
         return dot(r.astype(jnp.bfloat16), basis[...].reshape(order, n_coarse))
 
+    loads[0].wait()
+    ids[0] = own_map[...]
+    pl.semaphore_wait(barrier, chips + 5)
+    to_peers(ids, ids_sem, True)
+    send(inverse_h, inverse.at[core], inverse_sem, mate, j)
     loads[1].wait()
     loads[2].wait()
+    keep_coarse(0, on_basis(rhs[...]))
+    to_peers(coarse.at[0], coarse_sem.at[0])
     r_ref[...] = rhs[...]
     u_ref[...] = jnp.zeros_like(u_ref)
-    keep_coarse(0, on_basis(rhs[...]))
-    loads[0].wait()
-    ids[0] = own_map[...]
-
-    pl.semaphore_wait(barrier, chips + 5)
-    to_peers(ids, ids_sem)
-    send(inverse_h, inverse.at[core], inverse_sem, mate, j)
-    to_peers(coarse.at[0], coarse_sem.at[0])
 
     tiles[listed] = jnp.zeros_like(tiles[listed])
     permuted[6] = jnp.zeros_like(permuted[6])
@@ -266,7 +265,8 @@
             chosen = jnp.dot(
                 halves[...], jnp.concatenate(picks, axis=0), preferred_element_type=jnp.float32
             )
-            selected[a, :, t * LANES : (t + 2) * LANES] = chosen.astype(jnp.bfloat16)
+            start = pl.multiple_of((a * GROUP + t) * LANES, 2 * LANES)
+            selected[:, pl.ds(start, 2 * LANES)] = chosen.astype(jnp.bfloat16)
 
     near_to_far(ids, ids_sem, select)
     waiter(inverse_h, inverse_sem).wait_send()
@@ -278,14 +278,9 @@
         return jnp.concatenate([by_block[faces_s[0, f]] for f in range(6)], axis=1)
 
     def sweep(k, carry):
-        totals = []
-
-        def solve(a):
-            gathered = jnp.concatenate([coarse[k, a * GROUP + t] for t in range(GROUP)], axis=1)
-            totals.append(dot_nt(gathered, selected[a]))
-
-        near_to_far(coarse.at[k], coarse_sem.at[k], solve)
-        both = (totals[0] + totals[1]) + (totals[2] + totals[3])
+        waiter(coarse.at[k, pl.ds(1, chips - 1)], coarse_sem.at[k]).wait_recv()
+        gathered = jnp.concatenate([coarse[k, s] for s in range(chips)], axis=1)
+        both = dot_nt(gathered, selected[...])
         both = both[:, : 2 * held] + both[:, 2 * held :]
         mine = both[0:rights] + both[rights:]
         partial[k, 0] = mine
@@ -299,17 +294,11 @@
         numbers = own_map[...]
         lane, chip = numbers & (LANES - 1), numbers >> 7
         slot = ((z + groups - (chip >> 2)) & 3) * GROUP + ((x + GROUP - (chip & 3)) & 3)
-        found = [jnp.zeros((rights, LANES), jnp.float32)]
-
-        def collect(a):
-            own = found[-1]
-            for t in range(GROUP):
-                here = lanes_of(solved[k, a * GROUP + t].astype(jnp.float32), lane)
-                own = jnp.where(slot == a * GROUP + t, here, own)
-            found.append(own)
-
-        near_to_far(solved.at[k], solved_sem.at[k], collect)
-        own = found[-1].astype(jnp.bfloat16)
+        waiter(solved.at[k, pl.ds(1, chips - 1)], solved_sem.at[k]).wait_recv()
+        own = jnp.zeros((rights, LANES), jnp.float32)
+        for s in range(chips):
+            own = jnp.where(slot == s, lanes_of(solved[k, s].astype(jnp.float32), lane), own)
+        own = own.astype(jnp.bfloat16)
         u_faces = (base_faces + dot(own, face_basis_t[...])).astype(jnp.bfloat16)
         for f in range(6):
             faces_out[k, f] = u_faces[:, f * LANES : (f + 1) * LANES]
@@ -333,9 +322,9 @@
             jnp.where(face_on[b] == 6, here[:, b * LANES : (b + 1) * LANES], 0.0) for b in range(blocks)
         ]
         coarse_inside = on_basis(jnp.concatenate(inside, axis=1))
-        sent(coarse.at[k], coarse_sem.at[k])
+        waiter(coarse.at[k, pl.ds(1, chips - 1)], coarse_sem.at[k]).wait_send()
         waiter(partial.at[k, 0], partial_sem.at[k]).wait_send()
-        sent(solved.at[k], solved_sem.at[k])
+        waiter(solved.at[k, pl.ds(1, chips - 1)], solved_sem.at[k]).wait_send()
 
         waiter(faces_in.at[k], sems).wait_recv()
         coupling = [0.5 * lanes_of(faces_in[k, f].astype(jnp.float32), match[f]) for f in range(6)]
@@ -401,7 +390,7 @@
             vmem((2, held, coarse_all), f32),
             vmem((4 * held, coarse_all), bf16),
             vmem((order, order), bf16),
-            vmem((chips // GROUP, 4 * held, GROUP * n_coarse), bf16),
+            vmem((4 * held, chips * n_coarse), bf16),
             vmem((1, LANES), i32),
             pltpu.SMEM((1, LANES), i32),
             vmem((chips, 1, n_coarse), i32),
@@ -418,9 +407,9 @@
             dma,
             dma((2,)),
             dma((GROUP, 2)),
-            dma((SWEEPS, GROUP, 2)),
             dma((SWEEPS, 2)),
-            dma((SWEEPS, GROUP, 2)),
+            dma((SWEEPS, 2)),
+            dma((SWEEPS, 2)),
             dma((SWEEPS, 2)),
         ],
         compiler_params=pltpu.CompilerParams(

time: 69 us -> 68.1 us (0.987)
  Pallas kernels: 67.6 us -> 66.7 us
    pallas_call x1, Pallas kernels: 67.6 us -> 66.7 us  [body(): pl.pallas_call(functools.partial(kernel, subs, regs), out_shape=pltpu.VME...]
where the time goes in v4:
time: 68.1 us; the launch traced here: 67.9 us
  Pallas kernels  66.7 us (98%)
    pallas_call x1, Pallas kernels, body(): pl.pallas_call(functools.partial(kernel, subs, regs), out_shape=pltpu.VME...  66.7 us

profile of v4, /device:TPU:1, one launch (start us, length us, event | category | flops | bytes accessed | tf_op | source)
XLA Modules:
  0.0 67.9 jit_solution(11933044910754253972)
XLA Ops:
  0.6 66.7 %richardson.1 = bf16[2,16,1280]{2,1,0:T(8,128)(2,1)S(1)} custom-call(f32[16,1280]{1,0:T(8,128)} %bitcast.28, bf16[80,128,128]{2,1,0:T(8,128)(2,1)} %bitcast.25, s32[2,80]{1,0:T(2,128)} %bitcast.31, f32[1,1280]{1,0:T(1,128)} %bitcast.29, s32[1,6]{1,0:T(1,128)} %bitcast.32, s32[6,1,128]{2,1,0:T(1,128)} %bitcast.30, bf16[10,128,128]{2,1,0:T(8,128)(2,1)} %bitcast.27, ...), custom_call_target="tpu_custom_call" | custom-call | flops 188743680 | bytes 3670016 | tf_op jit(solution)/shard_map/richardson/pallas_call | solution.py:373
  67.3 0.6 slice_bitcast_fusion

commit v5 on v4

--- a/solution.py
+++ b/solution.py
@@ -92,7 +92,6 @@
     core = i % 2
     x, z = (i // 2) % GROUP, i // (2 * GROUP)
     mate = i + 1 - 2 * core
-    y = j % stride
     after, before = (i + 1) % subs, (i + subs - 1) % subs
     apart = (i + subs - 1 + 2 * core) % subs
 
@@ -304,18 +303,14 @@
             faces_out[k, f] = u_faces[:, f * LANES : (f + 1) * LANES]
         sems = face_sem.at[k]
 
-        def send_face(n, carry):
-            f = pick(n, (pick(y, (0, 3, 3, 1)), pick(y, (3, 2, 2, 3)), pick(y, (2, 1, 1, 2)), pick(y, (1, 0, 0, 0))))
-            by = pick(f, (regs - 1, 1, regs - stride, stride))
-            send(faces_out.at[k, f], faces_in.at[k, f + 1 - 2 * (f % 2)], sems, i, (j + by) % regs)
-            return carry
-
-        lax.fori_loop(0, 4, send_face, 0)
+        for f, by in ((1, 1), (0, regs - 1), (3, stride), (2, regs - stride)):
+            send(faces_out.at[k, f], faces_in.at[k, f ^ 1], sems, i, (j + by) % regs)
         send(faces_out.at[k, 4], faces_in.at[k, 5], sems, before, j)
         send(faces_out.at[k, 5], faces_in.at[k, 4], sems, after, j)
 
         u = base + dot(own, basis_t[...])
         u_ref[...] = u
+        result_o[0] = u.astype(result_o.dtype)
         here = rhs[...] - dot_nt(u.astype(jnp.bfloat16), dense[...])
         here_faces = faces_of(here)
         inside = [
@@ -337,12 +332,12 @@
 
         for f in range(6):
             permuted[f] = coupling[f]
-        r_ref[...] = here + jnp.concatenate([permuted[face_on[b]] for b in range(blocks)], axis=1)
+        r = here + jnp.concatenate([permuted[face_on[b]] for b in range(blocks)], axis=1)
+        r_ref[...] = r
+        result_o[1] = r.astype(result_o.dtype)
         return carry
 
     lax.fori_loop(0, SWEEPS, sweep, 0)
-    result_o[0] = u_ref[...].astype(result_o.dtype)
-    result_o[1] = r_ref[...].astype(result_o.dtype)
 
     for k in range(SWEEPS):
         waiter(faces_out.at[k], face_sem.at[k]).wait_send()

time: 68.1 us -> 68.1 us (level)
  no operation moved by 1% of the time
where the time goes in v5:
time: 68.1 us; the launch traced here: 68 us
  Pallas kernels  66.7 us (98%)
    pallas_call x1, Pallas kernels, body(): pl.pallas_call(functools.partial(kernel, subs, regs), out_shape=pltpu.VME...  66.7 us

profile of v5, /device:TPU:1, one launch (start us, length us, event | category | flops | bytes accessed | tf_op | source)
XLA Modules:
  0.0 68.0 jit_solution(10221641078426457380)
XLA Ops:
  0.6 66.7 %richardson.1 = bf16[2,16,1280]{2,1,0:T(8,128)(2,1)S(1)} custom-call(f32[16,1280]{1,0:T(8,128)} %bitcast.28, bf16[80,128,128]{2,1,0:T(8,128)(2,1)} %bitcast.25, s32[2,80]{1,0:T(2,128)} %bitcast.31, f32[1,1280]{1,0:T(1,128)} %bitcast.29, s32[1,6]{1,0:T(1,128)} %bitcast.32, s32[6,1,128]{2,1,0:T(1,128)} %bitcast.30, bf16[10,128,128]{2,1,0:T(8,128)(2,1)} %bitcast.27, ...), custom_call_target="tpu_custom_call" | custom-call | flops 188743680 | bytes 3670016 | tf_op jit(solution)/shard_map/richardson/pallas_call | solution.py:368
  67.4 0.6 slice_bitcast_fusion
